TPU v7x, 32 devices: a whole 2x2x4 slice. The times are simulated.
32 devices in a mesh: blk: 4 (over y, core), fsdp: 8 (over z, x).
Axes of the slice: x: 2, y: 2, z: 4, core: 2. Of those that a mesh axis runs over, the one named last changes fastest.
Arguments:
- img_feat: bfloat16 [2048, 1536], P(('blk', 'fsdp')), may hold values from -200 to 200
- txt_feat: bfloat16 [2048, 1152], P(('blk', 'fsdp')), may hold values from -200 to 200
- partner: int32 [2048], P(('blk', 'fsdp')), may hold values from 0 to 2047, as said below
- projection: bfloat16 [1536, 1152], P('fsdp'), may hold values from -0.4 to 2.9
- img_gain: float32 [1536], replicated, may hold values from 0.25 to 1.75
- txt_gain: float32 [1152], replicated, may hold values from 0.25 to 1.75
- log_scale: float32 [1], replicated, may hold values from 2.7 to 3.1
- logit_bias: float32 [1], replicated, may hold values from -11 to -9
Outputs:
- loss: float32 [1], replicated
- grad_log_scale: float32 [1], replicated
- grad_bias: float32 [1], replicated
- grad_proj: float32 [1536, 1152], P('fsdp')
- grad_img_gain: float32 [1536], replicated
- grad_txt_gain: float32 [1152], replicated
- grad_img_feat: float32 [2048, 1536], P(('blk', 'fsdp'))
- grad_txt_feat: float32 [2048, 1152], P(('blk', 'fsdp'))
Inputs may be any that keep to these rules, and one draw needn't show every extreme that they name: Each image's partner lies in the same aligned block of 64 rows, and every text is the partner of exactly one image.
All inputs are finite; a program needn't handle non-finite values.
Results may differ from a plain program's by a relative error of at most 0.0078.
Values may be sent and summed in bfloat16 or wider, within the bound.
A program may use at most 128 MiB of HBM per device.

v0:
```python
import jax
import jax.numpy as jnp
from jax import lax
from jax.sharding import PartitionSpec as P

EPSILON = 1e-06


def layer_norm(features):
    values = features.astype(jnp.float32)
    centered = values - jnp.mean(values, axis=1, keepdims=True)
    inverse = lax.rsqrt(jnp.mean(centered * centered, axis=1, keepdims=True) + EPSILON)
    return (centered * inverse, inverse)


def layer_norm_back(upstream, normed, inverse, gains):
    scaled = upstream * gains
    return inverse * (
        scaled
        - jnp.mean(scaled, axis=1, keepdims=True)
        - normed * jnp.mean(scaled * normed, axis=1, keepdims=True)
    )


def unit_rows(values):
    length = jnp.sqrt(jnp.sum(values * values, axis=1, keepdims=True) + EPSILON)
    return (values / length, length)


def unit_rows_back(upstream, values, length):
    product = jnp.sum(values * upstream, axis=1, keepdims=True)
    return upstream / length - values * product / (length * length * length)


def pair_terms(img_set, txt_set, targets, temper, offset, batch_total):
    similar = lax.dot_general(
        img_set, txt_set, (((1,), (1,)), ((), ())), preferred_element_type=jnp.float32
    )
    columns = lax.broadcasted_iota(jnp.int32, similar.shape, 1)
    labels = jnp.where(columns == targets[:, None], 1.0, -1.0).astype(jnp.float32)
    margin = labels * (temper * similar + offset)
    dlogit = -labels * jax.nn.sigmoid(-margin) / batch_total
    weighted = (temper * dlogit).astype(jnp.bfloat16)
    partial_sums = (
        jnp.sum(jax.nn.softplus(-margin)),
        jnp.sum(dlogit),
        jnp.sum(dlogit * temper * similar),
    )
    return (weighted, partial_sums)


def shards(img_feat, txt_feat, partner, projection, img_gain, txt_gain, log_scale, logit_bias):
    local_rows = img_feat.shape[0]
    group_count = lax.axis_size("blk")
    member_count = lax.axis_size("fsdp")
    batch_total = local_rows * group_count * member_count
    group_index = lax.axis_index("blk")
    member_index = lax.axis_index("fsdp")
    temper = jnp.exp(log_scale[0])
    offset = logit_bias[0]
    img_hat, img_inv = layer_norm(img_feat)
    img_norm = (img_hat * img_gain).astype(jnp.bfloat16)
    full_proj = lax.all_gather(projection, "fsdp", axis=0, tiled=True)
    img_proj = jnp.dot(img_norm, full_proj, preferred_element_type=jnp.float32)
    img_unit, img_len = unit_rows(img_proj)
    img_emb = img_unit.astype(jnp.bfloat16)
    txt_hat, txt_inv = layer_norm(txt_feat)
    txt_scaled = txt_hat * txt_gain
    txt_unit, txt_len = unit_rows(txt_scaled)
    txt_emb = txt_unit.astype(jnp.bfloat16)
    own_offsets = partner - (group_index * member_count + member_index) * local_rows
    txt_set = lax.all_gather(txt_emb, "fsdp", axis=0, tiled=True)
    block_targets = own_offsets + member_index * local_rows
    block_rows = img_emb.shape[0]
    set_rows = group_count * block_rows
    img_set = lax.all_gather(img_emb, "blk", axis=0, tiled=True)
    targets = jnp.full((set_rows,), -1, jnp.int32)
    targets = lax.dynamic_update_slice(targets, block_targets, (group_index * block_rows,))
    weighted, partial_sums = pair_terms(img_set, txt_set, targets, temper, offset, batch_total)
    grad_block = lax.psum_scatter(
        jnp.dot(weighted, txt_set, preferred_element_type=jnp.float32),
        "blk",
        scatter_dimension=0,
        tiled=True,
    )
    grad_txt_emb = lax.psum_scatter(
        lax.dot_general(
            weighted, img_set, (((0,), (0,)), ((), ())), preferred_element_type=jnp.float32
        ),
        "fsdp",
        scatter_dimension=0,
        tiled=True,
    )
    grad_img_proj = unit_rows_back(grad_block, img_proj, img_len).astype(jnp.bfloat16)
    grad_proj = lax.psum_scatter(
        lax.dot_general(
            img_norm, grad_img_proj, (((0,), (0,)), ((), ())), preferred_element_type=jnp.float32
        ),
        "fsdp",
        scatter_dimension=0,
        tiled=True,
    )
    grad_proj = lax.psum(grad_proj, "blk")
    grad_img_norm = lax.dot_general(
        grad_img_proj, full_proj, (((1,), (1,)), ((), ())), preferred_element_type=jnp.float32
    )
    grad_img_feat = layer_norm_back(grad_img_norm, img_hat, img_inv, img_gain)
    grad_txt_scaled = unit_rows_back(grad_txt_emb, txt_scaled, txt_len)
    grad_txt_feat = layer_norm_back(grad_txt_scaled, txt_hat, txt_inv, txt_gain)
    totals = lax.psum(
        (
            partial_sums[0],
            partial_sums[1],
            partial_sums[2],
            jnp.sum(grad_img_norm * img_hat, axis=0),
            jnp.sum(grad_txt_scaled * txt_hat, axis=0),
        ),
        ("blk", "fsdp"),
    )
    return (
        (totals[0] / batch_total).reshape(1),
        totals[2].reshape(1),
        totals[1].reshape(1),
        grad_proj,
        totals[3],
        totals[4],
        grad_img_feat,
        grad_txt_feat,
    )


def solution(mesh):
    placed = (
        P(("blk", "fsdp"), None),
        P(("blk", "fsdp"), None),
        P(("blk", "fsdp")),
        P("fsdp", None),
        P(),
        P(),
        P(),
        P(),
    )
    return jax.shard_map(
        shards,
        mesh=mesh,
        in_specs=placed,
        out_specs=(
            P(),
            P(),
            P(),
            P("fsdp", None),
            P(),
            P(),
            P(("blk", "fsdp"), None),
            P(("blk", "fsdp"), None),
        ),
        check_vma=False,
    )
```

profile of v0, /device:TPU:17, one launch (start us, length us, event | category | flops | bytes accessed | tf_op | source)
XLA Modules:
  0.0 399.9 jit_solution(4606676077515650511)
XLA Ops:
  7.2 0.0 all-gather.3.cloned.1.call-start
  7.2 0.7 all-gather.3.cloned.1.call-update
  7.9 0.0 all-gather.5.cloned.1.call-start
  7.9 1.0 convert_reduce_fusion.1
  9.0 1.1 fusion.33
  10.1 1.1 fusion.24
  11.3 1.7 fusion.25
  13.0 0.0 all-gather.5.cloned.1.call-update
  13.0 0.0 reduce-scatter.4.cloned.1.call-start
  13.1 1.1 convert_reduce_fusion
  15.5 1.1 fusion.13
  16.7 0.8 add_dynamic-update-slice_fusion
  17.4 57.7 %all-gather.3.cloned.1.call-done = bf16[1536,1152]{1,0:T(8,128)(2,1)} async-done(((bf16[192,1152]{1,0:T(8,128)(2,1)}), bf16[1536,1152]{1,0:T(8,128)(2,1)}) %all-gather.3.cloned.1.call-update) | async-done | bytes 3538960 | tf_op jit(solution)/shard_map/all_gather | solution.py:63
  75.2 3.0 multiply_reduce_fusion.4
  78.2 0.1 divide_convert_fusion
  78.3 8.7 %all_gather.10 = bf16[256,1152]{1,0:T(8,128)(2,1)S(1)} all-gather(bf16[64,1152]{1,0:T(8,128)(2,1)S(1)} %divide_convert_fusion), channel_id=1, replica_groups=mesh['blk'=4,'fsdp'=8] {'blk'}, dimensions={0}, use_global_device_ids=true | all-gather | bytes 737280 | tf_op jit(solution)/shard_map/all_gather | solution.py:76
  87.0 29.9 %all-gather.5.cloned.1.call-done = bf16[512,1152]{1,0:T(8,128)(2,1)} async-done(((bf16[64,1152]{1,0:T(8,128)(2,1)}), bf16[512,1152]{1,0:T(8,128)(2,1)}) %all-gather.5.cloned.1.call-update) | async-done | bytes 1179664 | tf_op jit(solution)/shard_map/all_gather | solution.py:72
  117.0 0.0 copy-start.5
  117.0 3.1 multiply_reduce_fusion
  120.0 0.0 copy-done.5
  120.0 1.7 fusion.35
  121.7 0.0 reduce-scatter.4.cloned.1.call-update
  121.7 0.0 reduce-scatter.8.cloned.1.call-start
  121.8 2.2 fusion.34
  123.9 0.0 copy-start.1
  123.9 0.0 copy-start.4
  123.9 0.0 reduce-scatter.8.cloned.1.call-update
  124.0 0.0 reduce-scatter.6.cloned.1.call-start
  124.0 24.2 %reduce-scatter.4.cloned.1.call-done = f32[64,1152]{1,0:T(8,128)} async-done(((f32[256,1152]{1,0:T(8,128)}), f32[64,1152]{1,0:T(8,128)}) %reduce-scatter.4.cloned.1.call-update) | async-done | bytes 294928 | tf_op jit(solution)/shard_map/reduce_scatter | solution.py:80
  148.2 1.1 multiply_reduce_fusion.3
  149.3 0.0 copy-done.1
  149.3 0.0 copy-done.4
  149.3 5.1 %fusion.36 = f32[1536,1152]{1,0:T(8,128)} fusion(bf16[64,1536]{1,0:T(8,128)(2,1)S(1)} %copy-done.1, f32[1536]{0:T(1024)S(1)} %copy-done.4, f32[64]{0:T(128)S(1)} %add_rsqrt_fusion.1, f32[64]{0:T(128)S(1)} %broadcast_multiply_fusion.5, f32[64,1152]{1,0:T(8,128)S(1)} %get-tuple-element.28, f32[64,1152]{1,0:T(8,128)} %reduce-scatter.4.cloned.1.call-done, ...), kind=kOutput, calls=%fused_computation.66 | convolution fusion | flops 227352576 | bytes 7871744 | tf_op jit(solution)/shard_map/dot_general | solution.py:96
  154.4 0.0 copy-start.2
  154.4 0.0 reduce-scatter.6.cloned.1.call-update
  154.4 0.0 copy-start
  154.4 0.0 copy-start.3
  154.4 0.0 all-reduce.3.cloned.1.call-start
  154.5 0.9 copy-done.2
  155.4 3.3 fusion.10
  158.7 0.9 fusion.12
  159.6 58.8 %reduce-scatter.8.cloned.1.call-done = f32[64,1152]{1,0:T(8,128)} async-done(((f32[512,1152]{1,0:T(8,128)}), f32[64,1152]{1,0:T(8,128)}) %reduce-scatter.8.cloned.1.call-update) | async-done | bytes 294928 | tf_op jit(solution)/shard_map/reduce_scatter | solution.py:86
  218.4 0.0 copy-done
  218.4 0.0 copy-done.3
  218.4 1.2 fusion.26
  219.6 1.3 fusion.30
  220.9 45.2 %all-reduce = (f32[]{:T(128)}, f32[1]{0:T(128)}, f32[1]{0:T(128)}, f32[1536]{0:T(1024)}, f32[1152]{0:T(1024)}) all-reduce(f32[]{:T(128)} %get-tuple-element.12, f32[1]{0:T(128)} %bitcast.3, f32[1]{0:T(128)} %bitcast.4, f32[1536]{0:T(1024)S(1)} %get-tuple-element.9, ...), channel_id=1, replica_groups=mesh['blk'=4,'fsdp'=8] {'blk','fsdp'}, use_global_device_ids=true, to_apply=%region_7.8 | all-reduce | flops 2691 | bytes 21528 | tf_op jit(solution)/shard_map/psum | solution.py:110
  266.8 86.8 %reduce-scatter.6.cloned.1.call-done = f32[192,1152]{1,0:T(8,128)} async-done(((f32[1536,1152]{1,0:T(8,128)}), f32[192,1152]{1,0:T(8,128)}) %reduce-scatter.6.cloned.1.call-update) | async-done | bytes 884752 | tf_op jit(solution)/shard_map/reduce_scatter | solution.py:95
  353.5 0.0 all-reduce.3.cloned.1.call-update
  353.6 0.9 fusion.32
  354.4 35.4 %all-reduce.3.cloned.1.call-done = f32[192,1152]{1,0:T(8,128)} async-done(((f32[192,1152]{1,0:T(8,128)}), f32[192,1152]{1,0:T(8,128)}) %all-reduce.3.cloned.1.call-update) | async-done | bytes 884752 | tf_op jit(solution)/shard_map/psum | solution.py:103
  389.8 2.1 copy.20
  (9 shorter events, 0.0 us)
Async XLA Ops:
  7.2 68.0 %all-gather.3.cloned.1.call-start = ((), (), s32[]{:S(2)}) async-start(), calls=%async_computation.3 | async-start | bytes 3981312 | tf_op jit(solution)/shard_map/all_gather | solution.py:63
  7.9 109.1 %all-gather.5.cloned.1.call-start = ((), (), s32[]{:S(2)}) async-start(), calls=%async_computation.4 | async-start | bytes 1327104 | tf_op jit(solution)/shard_map/all_gather | solution.py:72
  13.0 135.2 %reduce-scatter.4.cloned.1.call-start = ((), (), s32[]{:S(2)}) async-start(), calls=%async_computation.5 | async-start | bytes 1474560 | tf_op jit(solution)/shard_map/reduce_scatter | solution.py:80
  117.0 3.1 copy-start.5
  121.7 96.7 %reduce-scatter.8.cloned.1.call-start = ((), (), s32[]{:S(2)}) async-start(), calls=%async_computation.8 | async-start | bytes 2654208 | tf_op jit(solution)/shard_map/reduce_scatter | solution.py:86
  123.9 25.4 %copy-start.1 = (bf16[64,1536]{1,0:T(8,128)(2,1)S(1)}, bf16[64,1536]{1,0:T(8,128)(2,1)}, u32[]{:S(2)}) copy-start(bf16[64,1536]{1,0:T(8,128)(2,1)} %param.8) | copy-start | bytes 589828
  123.9 25.4 %copy-start.4 = (f32[1536]{0:T(1024)S(1)}, f32[1536]{0:T(1024)}, u32[]{:S(2)}) copy-start(f32[1536]{0:T(1024)} %param.12) | copy-start | bytes 18436
  124.0 229.6 %reduce-scatter.6.cloned.1.call-start = ((), (), s32[]{:S(2)}) async-start(), calls=%async_computation.6 | async-start | bytes 7962624 | tf_op jit(solution)/shard_map/reduce_scatter | solution.py:95
  154.4 1.0 copy-start.2
  154.4 64.0 %copy-start = (bf16[64,1152]{1,0:T(8,128)(2,1)S(1)}, bf16[64,1152]{1,0:T(8,128)(2,1)}, u32[]{:S(2)}) copy-start(bf16[64,1152]{1,0:T(8,128)(2,1)} %param.9) | copy-start | bytes 442372
  154.4 64.0 %copy-start.3 = (f32[1152]{0:T(1024)S(1)}, f32[1152]{0:T(1024)}, u32[]{:S(2)}) copy-start(f32[1152]{0:T(1024)} %param.13) | copy-start | bytes 13828
  154.4 235.4 %all-reduce.3.cloned.1.call-start = ((), (), s32[]{:S(2)}) async-start(), calls=%async_computation.7 | async-start | bytes 1769472 | tf_op jit(solution)/shard_map/psum | solution.py:103
Sparse Core Ops, SparseCore 0:
  10.2 64.9 all-gather.2
  77.9 38.9 all-gather.4
  121.8 26.3 reduce-scatter.3
  152.0 66.4 reduce-scatter.7
  222.4 131.1 reduce-scatter.5
  355.8 33.9 all-reduce.2
where the time goes:
time: 403 us; the launch traced here: 400 us
  waiting for transfers between devices  293 us (73%)
  blocking collectives  53.9 us (13%)
  matrix products  18.3 us (5%)
  between operations  17.4 us (4%)
  other arithmetic  13.5 us (3%)
    reduce_scatter x1, waiting for transfers between devices, shards(): lax.psum_scatter(lax.dot_general(img_norm, grad_img_proj, (((0,), (0,)),...  86.8 us
    reduce_scatter x1, waiting for transfers between devices, shards(): lax.psum_scatter(lax.dot_general(weighted, img_set, (((0,), (0,)), ((), (...  58.8 us
    all_gather x1, waiting for transfers between devices, shards(): full_proj = lax.all_gather(projection, 'fsdp', axis=0, tiled=True)  57.7 us
    psum x1, blocking collectives, shards(): lax.psum((partial_sums[0], partial_sums[1], partial_sums[2], jnp.sum(grad...  45.2 us
    psum x1, waiting for transfers between devices, shards(): grad_proj = lax.psum(grad_proj, 'blk')  35.4 us
    all_gather x1, waiting for transfers between devices, shards(): txt_set = lax.all_gather(txt_emb, 'fsdp', axis=0, tiled=True)  29.9 us
    reduce_scatter x1, waiting for transfers between devices, shards(): lax.psum_scatter(jnp.dot(weighted, txt_set, preferred_element_type=jnp.fl...  24.2 us
    all_gather x1, blocking collectives, shards(): img_set = lax.all_gather(img_emb, 'blk', axis=0, tiled=True)  8.72 us
  transfers between devices with their start and end apart: 6, of which 6 were waited for; matrix products, arithmetic and copies ran while one was open for 7% of the time, Pallas kernels for 0%

commit v1 on v0

--- a/solution.py
+++ b/solution.py
@@ -1,6 +1,10 @@
+import functools
+
 import jax
 import jax.numpy as jnp
 from jax import lax
+from jax.experimental import pallas as pl
+from jax.experimental.pallas import tpu as pltpu
 from jax.sharding import PartitionSpec as P
 
 EPSILON = 1e-06
@@ -129,6 +133,396 @@
     )
 
 
+MESH = pl.DeviceIdType.MESH
+BF16 = jnp.bfloat16
+F32 = jnp.float32
+
+
+def txt_slot(distance):
+    return distance // 2 if distance % 2 else 4 + distance // 2
+
+
+def flip(bit, yes):
+    return 1 - bit if yes else bit
+
+
+def matmul(left, right):
+    return jnp.dot(left, right, preferred_element_type=F32)
+
+
+def matmul_nt(left, right):
+    return lax.dot_general(left, right, (((1,), (1,)), ((), ())), preferred_element_type=F32)
+
+
+def pair_math(similar, labels, temper, offset, batch_total):
+    margin = labels * (temper * similar + offset)
+    small = jnp.exp(-jnp.abs(margin))
+    chance = jnp.where(margin >= 0.0, small, 1.0) / (1.0 + small)
+    dlogit = -labels * chance / batch_total
+    softplus = jnp.maximum(-margin, 0.0) + jnp.log1p(small)
+    return dlogit, softplus
+
+
+def total(values):
+    return jnp.sum(jnp.sum(values, axis=0, keepdims=True), axis=1, keepdims=True)
+
+
+def kernel(
+    batch_total, img_ref, txt_ref, goal_ref, part_ref, igain_ref, tgain_ref, scale_ref, bias_ref,
+    loss_ref, gscale_ref, gbias_ref, gproj_ref, gig_ref, gtg_ref, gif_ref, gtf_ref,
+    full_ref, norm_ref, hat_ref, turned_ref, turned_in, proj_ref,
+    txt_set, img_set, weight_ref, turnw_ref, block_ref, block_out, block_in,
+    gtx_ref, gtx_out, gtx_in, gtz_out, gtz_in, grad_set,
+    gp_in, gp_out, gp_far, gp_sum, gp_end, small_ref, small_in, mid_ref, mid_in, send_sem, recv_sem,
+):
+    rows = img_ref.shape[0]
+    depth = part_ref.shape[0]
+    quarter = depth // 4
+    half = depth // 2
+    b = lax.axis_index("blk")
+    f = lax.axis_index("fsdp")
+    core, y = b % 2, b // 2
+    x, z_low, z_high = f % 2, (f // 2) % 2, f // 4
+
+    def member(r):
+        return (flip(z_high, r & 4) * 2 + flip(z_low, r & 2)) * 2 + flip(x, r & 1)
+
+    def group(r):
+        return flip(y, r & 2) * 2 + flip(core, r & 1)
+
+    barrier = pltpu.get_barrier_semaphore()
+    for r in range(1, 8):
+        pl.semaphore_signal(barrier, inc=1, device_id=(b, member(r)), device_id_type=MESH)
+    for r in range(1, 4):
+        pl.semaphore_signal(barrier, inc=1, device_id=(group(r), f), device_id_type=MESH)
+    pl.semaphore_wait(barrier, 10)
+
+    copies = []
+
+    def send(source, target, to):
+        k = len(copies)
+        copy = pltpu.make_async_remote_copy(
+            src_ref=source, dst_ref=target, send_sem=send_sem.at[k], recv_sem=recv_sem.at[k],
+            device_id=to, device_id_type=MESH,
+        )
+        copy.start()
+        copies.append(copy)
+        return copy
+
+    def along(r):
+        return (b, member(r))
+
+    def across(r):
+        return (group(r), f)
+
+    def piece(r, q):
+        start = member(r) * depth + group(q) * quarter
+        return full_ref.at[pl.ds(pl.multiple_of(start, 16), quarter), :]
+
+    own_piece = part_ref.at[pl.ds(pl.multiple_of(b * quarter, 16), quarter), :]
+    arrive = {}
+    for r in (4, 6, 2, 1):
+        arrive[r, 0] = send(own_piece, piece(0, 0), along(r))
+    full_ref[pl.ds(pl.multiple_of(f * depth, 16), depth), :] = part_ref[...]
+
+    values = txt_ref[...].astype(F32)
+    centered = values - jnp.mean(values, axis=1, keepdims=True)
+    txt_inv = lax.rsqrt(jnp.mean(centered * centered, axis=1, keepdims=True) + EPSILON)
+    txt_hat = centered * txt_inv
+    txt_scaled = txt_hat * tgain_ref[...]
+    txt_len = jnp.sqrt(jnp.sum(txt_scaled * txt_scaled, axis=1, keepdims=True) + EPSILON)
+    txt_set[txt_slot(0)] = (txt_scaled / txt_len).astype(BF16)
+    txt_arrive = {}
+    for r in (4, 6, 2, 1):
+        txt_arrive[r] = send(txt_set.at[txt_slot(0)], txt_set.at[txt_slot(r)], along(r))
+
+    values = img_ref[...].astype(F32)
+    centered = values - jnp.mean(values, axis=1, keepdims=True)
+    img_inv = lax.rsqrt(jnp.mean(centered * centered, axis=1, keepdims=True) + EPSILON)
+    img_hat = centered * img_inv
+    hat_ref[...] = img_hat
+    img_norm = img_hat * igain_ref[...]
+    norm_ref[...] = img_norm.astype(BF16)
+    turned_ref[...] = jnp.transpose(img_norm).astype(BF16)
+
+    for r in (2, 4, 6):
+        arrive[r, 0].wait_recv()
+        arrive[r + 1, 0] = send(piece(r, 0), piece(r, 0), along(1))
+        arrive[r, 2] = send(piece(r, 0), piece(r, 0), across(2))
+        arrive[r, 1] = send(piece(r, 0), piece(r, 0), across(1))
+    for r in (1, 3, 5, 7):
+        arrive[r, 0].wait_recv()
+        arrive[r, 2] = send(piece(r, 0), piece(r, 0), across(2))
+        arrive[r, 1] = send(piece(r, 0), piece(r, 0), across(1))
+    for r in (2, 4, 6):
+        txt_arrive[r].wait_recv()
+        txt_arrive[r + 1] = send(
+            txt_set.at[txt_slot(r)], txt_set.at[txt_slot(r + 1)], along(1)
+        )
+    for r in (2, 4, 6, 1, 3, 5, 7):
+        arrive[r, 2].wait_recv()
+        arrive[r, 3] = send(piece(r, 2), piece(r, 2), across(1))
+    img_proj = None
+    for r in (0, 2, 4, 6):
+        for s in (r, r + 1):
+            if s:
+                arrive[s, 1].wait_recv()
+                arrive[s, 3].wait_recv()
+        pair = member(r) // 2 * (2 * depth)
+        pair = pl.ds(pl.multiple_of(pair, 128), 2 * depth)
+        term = matmul(norm_ref[:, pair], full_ref[pair, :])
+        img_proj = term if img_proj is None else img_proj + term
+    proj_ref[...] = img_proj
+    img_len = jnp.sqrt(jnp.sum(img_proj * img_proj, axis=1, keepdims=True) + EPSILON)
+    img_set[0:rows] = (img_proj / img_len).astype(BF16)
+    own = img_set.at[0:rows]
+    from_y = send(own, img_set.at[2 * rows:3 * rows], across(2))
+    from_core = send(own, img_set.at[rows:2 * rows], across(1))
+    turned_arrive = {}
+    for r in (2, 4, 6, 1, 3, 5, 7):
+        rows_of = pl.ds(pl.multiple_of(member(r) * depth, 16), depth)
+        turned_arrive[r] = send(turned_ref.at[rows_of, :], turned_in.at[r], along(r))
+    turned_in[0] = turned_ref[pl.ds(pl.multiple_of(f * depth, 16), depth), :]
+
+    for r in (1, 3, 5, 7):
+        txt_arrive[r].wait_recv()
+    txt_all = txt_set[...].reshape(8 * rows, txt_set.shape[2])
+    temper = jnp.exp(scale_ref[...])
+    offset = bias_ref[...]
+    similar = matmul_nt(img_set[0:rows], txt_all)
+    columns = lax.broadcasted_iota(jnp.int32, similar.shape, 1)
+    goal = goal_ref[...] - (b * 8 + f) * rows + txt_slot(0) * rows
+    labels = jnp.where(columns == goal, 1.0, -1.0).astype(F32)
+    dlogit, softplus = pair_math(similar, labels, temper, offset, batch_total)
+    weighted = temper * dlogit
+    weight_ref[0:rows] = weighted.astype(BF16)
+    turnw_ref[:, 0:rows] = jnp.transpose(weighted).astype(BF16)
+    loss = total(softplus)
+    grad_bias = total(dlogit)
+    grad_scale = total(weighted * similar)
+    from_y.wait_recv()
+    from_far = send(img_set.at[2 * rows:3 * rows], img_set.at[3 * rows:4 * rows], across(1))
+    from_core.wait_recv()
+    from_far.wait_recv()
+    similar = matmul_nt(img_set[rows:4 * rows], txt_all)
+    dlogit, softplus = pair_math(similar, -1.0, temper, offset, batch_total)
+    weighted = temper * dlogit
+    weight_ref[rows:4 * rows] = weighted.astype(BF16)
+    block = matmul(weight_ref[...], txt_all)
+    block_out[0] = block[rows:2 * rows].astype(BF16)
+    block_out[1] = block[3 * rows:4 * rows].astype(BF16)
+    near = send(block_out.at[0], block_in.at[0], across(1))
+    far = send(block_out.at[1], block_in.at[1], across(1))
+    block_ref[0] = block[0:rows]
+    block_ref[1] = block[2 * rows:3 * rows]
+    turnw_ref[:, rows:4 * rows] = jnp.transpose(weighted).astype(BF16)
+    loss = loss + total(softplus)
+    grad_bias = grad_bias + total(dlogit)
+    grad_scale = grad_scale + total(weighted * similar)
+    far.wait_recv()
+    block_out[2] = (block_ref[1] + block_in[1].astype(F32)).astype(BF16)
+    wide = send(block_out.at[2], block_in.at[2], across(2))
+
+    odd = matmul(turnw_ref[0:4 * rows], img_set[...]).astype(BF16)
+    gtx_out[...] = odd.reshape(gtx_out.shape)
+    gtx_arrive = [
+        send(gtx_out.at[k], gtx_in.at[k], along(1)) for k in (1, 2, 3, 0)
+    ]
+    gtx_ref[...] = matmul(turnw_ref[4 * rows:8 * rows], img_set[...]).reshape(gtx_ref.shape)
+
+    near.wait_recv()
+    wide.wait_recv()
+    img_proj = proj_ref[...]
+    grad = block_ref[0] + block_in[0].astype(F32) + block_in[2].astype(F32)
+    product = jnp.sum(img_proj * grad, axis=1, keepdims=True)
+    grad = grad / img_len - img_proj * product / (img_len * img_len * img_len)
+    grad_set[0] = grad.astype(BF16)
+    grad_arrive = {}
+    for r in (4, 6, 2, 1):
+        grad_arrive[r] = send(grad_set.at[0], grad_set.at[r], along(r))
+
+    gtz_arrive = {}
+    for k in (1, 2, 3):
+        gtx_arrive[k - 1].wait_recv()
+        gtz_out[k] = (gtx_ref[k] + gtx_in[k].astype(F32)).astype(BF16)
+        gtz_arrive[k] = send(gtz_out.at[k], gtz_in.at[k], along(2 * k))
+
+    grad_norm = matmul_nt(grad_set[0], full_ref[...])
+    img_hat = hat_ref[...]
+    img_gain_sum = jnp.sum(grad_norm * img_hat, axis=0, keepdims=True)
+    scaled = grad_norm * igain_ref[...]
+    gif_ref[...] = img_inv * (
+        scaled
+        - jnp.mean(scaled, axis=1, keepdims=True)
+        - img_hat * jnp.mean(scaled * img_hat, axis=1, keepdims=True)
+    )
+
+    for r in (2, 4, 6):
+        grad_arrive[r].wait_recv()
+        grad_arrive[r + 1] = send(grad_set.at[r], grad_set.at[r + 1], along(1))
+
+    grad_proj = matmul(turned_in[0], grad_set[0])
+    for r in (2, 4, 6):
+        turned_arrive[r].wait_recv()
+        grad_proj = grad_proj + matmul(turned_in[r], grad_set[r])
+
+    gtx_arrive[3].wait_recv()
+    grad = gtx_ref[0] + gtx_in[0].astype(F32)
+    for k in (1, 2, 3):
+        gtz_arrive[k].wait_recv()
+        grad = grad + gtz_in[k].astype(F32)
+    product = jnp.sum(txt_scaled * grad, axis=1, keepdims=True)
+    grad = grad / txt_len - txt_scaled * product / (txt_len * txt_len * txt_len)
+    txt_gain_sum = jnp.sum(grad * txt_hat, axis=0, keepdims=True)
+    img_tiles = img_ref.shape[1] // 128
+    txt_tiles = txt_ref.shape[1] // 128
+    small_ref[...] = jnp.zeros_like(small_ref)
+    for k in range(img_tiles):
+        small_ref[k:k + 1, :] = img_gain_sum[:, k * 128:(k + 1) * 128]
+    for k in range(txt_tiles):
+        at = img_tiles + k
+        small_ref[at:at + 1, :] = txt_gain_sum[:, k * 128:(k + 1) * 128]
+    at = img_tiles + txt_tiles
+    lanes = lax.broadcasted_iota(jnp.int32, (1, 128), 1)
+    small_ref[at:at + 1, :] = jnp.where(
+        lanes == 0, loss, jnp.where(lanes == 1, grad_scale, jnp.where(lanes == 2, grad_bias, 0.0))
+    )
+    small_arrive = [send(small_ref, small_in.at[b], across(r)) for r in (1, 2, 3)]
+
+    scaled = grad * tgain_ref[...]
+    gtf_ref[...] = txt_inv * (
+        scaled
+        - jnp.mean(scaled, axis=1, keepdims=True)
+        - txt_hat * jnp.mean(scaled * txt_hat, axis=1, keepdims=True)
+    )
+
+    for r in (1, 3, 5, 7):
+        turned_arrive[r].wait_recv()
+        grad_arrive[r].wait_recv()
+        grad_proj = grad_proj + matmul(turned_in[r], grad_set[r])
+    gproj_ref[...] = grad_proj
+    mine = pl.ds(pl.multiple_of(core * half, 16), half)
+    other = pl.ds(pl.multiple_of((1 - core) * half, 16), half)
+    gp_first = send(gproj_ref.at[other, :], gp_in, across(1))
+
+    small_in[b] = small_ref[...]
+    for copy in small_arrive:
+        copy.wait_recv()
+    mid_ref[...] = (small_in[0] + small_in[1]) + (small_in[2] + small_in[3])
+    mid_arrive = [send(mid_ref, mid_in.at[f], along(r)) for r in range(1, 8)]
+    mid_in[f] = mid_ref[...]
+
+    gp_first.wait()
+    gp_out[...] = (gproj_ref[mine, :] + gp_in[...]).astype(BF16)
+    gp_step = send(gp_out, gp_far, across(2))
+
+    for copy in mid_arrive:
+        copy.wait_recv()
+    sums = mid_in[0]
+    for k in range(1, 8):
+        sums = sums + mid_in[k]
+    for k in range(img_tiles):
+        gig_ref[:, k * 128:(k + 1) * 128] = sums[k:k + 1, :]
+    for k in range(txt_tiles):
+        at = img_tiles + k
+        gtg_ref[:, k * 128:(k + 1) * 128] = sums[at:at + 1, :]
+    at = img_tiles + txt_tiles
+    loss_ref[...] = sums[at:at + 1, 0:1] / batch_total
+    gscale_ref[...] = sums[at:at + 1, 1:2]
+    gbias_ref[...] = sums[at:at + 1, 2:3]
+
+    gp_step.wait_recv()
+    gp_sum[...] = gp_out[...].astype(F32) + gp_far[...].astype(F32)
+    gp_last = send(gp_sum, gp_end, across(1))
+    gproj_ref[mine, :] = gp_sum[...]
+    gp_last.wait_recv()
+    gproj_ref[other, :] = gp_end[...]
+
+    for copy in copies:
+        if copy is not gp_first:
+            copy.wait_send()
+
+
+def fused_shards(img_feat, txt_feat, partner, projection, img_gain, txt_gain, log_scale, logit_bias):
+    rows, width = img_feat.shape
+    emb = txt_feat.shape[1]
+    depth = projection.shape[0]
+    batch_total = rows * lax.axis_size("blk") * lax.axis_size("fsdp")
+    small_rows = -(-((width + emb) // 128 + 1) // 8) * 8
+    scalar = jax.ShapeDtypeStruct((1, 1), F32)
+    vmem = pltpu.VMEM
+    outs = pl.pallas_call(
+        functools.partial(kernel, batch_total),
+        out_shape=(
+            scalar,
+            scalar,
+            scalar,
+            jax.ShapeDtypeStruct((depth, emb), F32),
+            jax.ShapeDtypeStruct((1, width), F32),
+            jax.ShapeDtypeStruct((1, emb), F32),
+            jax.ShapeDtypeStruct((rows, width), F32),
+            jax.ShapeDtypeStruct((rows, emb), F32),
+        ),
+        in_specs=[pl.BlockSpec(memory_space=vmem)] * 8,
+        out_specs=tuple([pl.BlockSpec(memory_space=vmem)] * 8),
+        scratch_shapes=[
+            vmem((width, emb), BF16),
+            vmem((rows, width), BF16),
+            vmem((rows, width), F32),
+            vmem((width, rows), BF16),
+            vmem((8, depth, rows), BF16),
+            vmem((rows, emb), F32),
+            vmem((8, rows, emb), BF16),
+            vmem((4 * rows, emb), BF16),
+            vmem((4 * rows, 8 * rows), BF16),
+            vmem((8 * rows, 4 * rows), BF16),
+            vmem((2, rows, emb), F32),
+            vmem((3, rows, emb), BF16),
+            vmem((3, rows, emb), BF16),
+            vmem((4, rows, emb), F32),
+            vmem((4, rows, emb), BF16),
+            vmem((4, rows, emb), BF16),
+            vmem((4, rows, emb), BF16),
+            vmem((4, rows, emb), BF16),
+            vmem((8, rows, emb), BF16),
+            vmem((depth // 2, emb), F32),
+            vmem((depth // 2, emb), BF16),
+            vmem((depth // 2, emb), BF16),
+            vmem((depth // 2, emb), F32),
+            vmem((depth // 2, emb), F32),
+            vmem((small_rows, 128), F32),
+            vmem((4, small_rows, 128), F32),
+            vmem((small_rows, 128), F32),
+            vmem((8, small_rows, 128), F32),
+            pltpu.SemaphoreType.DMA((80,)),
+            pltpu.SemaphoreType.DMA((80,)),
+        ],
+        compiler_params=pltpu.CompilerParams(
+            collective_id=0, has_side_effects=True, vmem_limit_bytes=48 * 1024 * 1024
+        ),
+    )(
+        img_feat,
+        txt_feat,
+        partner.reshape(rows, 1),
+        projection,
+        img_gain.reshape(1, width),
+        txt_gain.reshape(1, emb),
+        log_scale.reshape(1, 1),
+        logit_bias.reshape(1, 1),
+    )
+    loss, grad_scale, grad_bias, grad_proj, img_sum, txt_sum, img_grad, txt_grad = outs
+    return (
+        loss.reshape(1),
+        grad_scale.reshape(1),
+        grad_bias.reshape(1),
+        grad_proj,
+        img_sum.reshape(width),
+        txt_sum.reshape(emb),
+        img_grad,
+        txt_grad,
+    )
+
+
 def solution(mesh):
     placed = (
         P(("blk", "fsdp"), None),
@@ -140,8 +534,9 @@
         P(),
         P(),
     )
+    fused = mesh.shape["blk"] == 4 and mesh.shape["fsdp"] == 8
     return jax.shard_map(
-        shards,
+        fused_shards if fused else shards,
         mesh=mesh,
         in_specs=placed,
         out_specs=(

time: 403 us -> 103 us (0.26)
  waiting for transfers between devices: 293 us -> 0 us
  Pallas kernels: 0 us -> 87.1 us
  blocking collectives: 53.9 us -> 0 us
  matrix products: 18.3 us -> 0 us
  other arithmetic: 13.5 us -> 1.24 us
  between operations: 17.4 us -> 7.25 us
    reduce_scatter x3 -> x0, waiting for transfers between devices: 170 us -> none  [the longest x1 86.8 us: shards(): lax.psum_scatter(lax.dot_general(img_norm, grad_img_proj, (((0,), (0,)),...]
    all_gather x2 -> x0, waiting for transfers between devices: 87.7 us -> none  [the longest x1 57.7 us: shards(): full_proj = lax.all_gather(projection, 'fsdp', axis=0, tiled=True)]
    pallas_call x0 -> x1, Pallas kernels: none -> 87.1 us  [fused_shards(): pl.pallas_call(functools.partial(kernel, batch_total), out_shape=(scalar,...]
    psum x1 -> x0, blocking collectives: 45.2 us -> none  [shards(): lax.psum((partial_sums[0], partial_sums[1], partial_sums[2], jnp.sum(grad...]
    psum x1 -> x0, waiting for transfers between devices: 35.4 us -> none  [shards(): grad_proj = lax.psum(grad_proj, 'blk')]
    dot_general x6 -> x0, matrix products: 18.3 us -> none  [the longest x1 5.08 us: shards(): lax.dot_general(img_norm, grad_img_proj, (((0,), (0,)), ((), ())), prefer...]
    reduce_sum x8 -> x0, other arithmetic: 9.07 us -> none  [the longest x2 2.27 us: unit_rows_back(): product = jnp.sum(values * upstream, axis=1, keepdims=True)]
    all_gather x1 -> x0, blocking collectives: 8.72 us -> none  [shards(): img_set = lax.all_gather(img_emb, 'blk', axis=0, tiled=True)]
  transfers between devices with their start and end apart: 6 -> 0, of which waited for: 6 -> 0; matrix products, arithmetic and copies ran while one was open for 7% -> 0% of each run, Pallas kernels for 0% -> 0%
where the time goes in v1:
time: 103 us; the launch traced here: 102 us
  Pallas kernels  87.1 us (85%)
  between operations  7.25 us (7%)
  local copies, waits for them, and re-layouts  6.65 us (6%)
  other arithmetic  1.24 us (1%)
    pallas_call x1, Pallas kernels, fused_shards(): pl.pallas_call(functools.partial(kernel, batch_total), out_shape=(scalar,...  87.1 us
    unnamed x15, local copies, waits for them, and re-layouts  6.54 us

profile of v1, /device:TPU:17, one launch (start us, length us, event | category | flops | bytes accessed | tf_op | source)
XLA Modules:
  0.0 102.2 jit_solution(2205071724504039864)
XLA Ops:
  0.6 0.0 copy-start.4
  1.9 0.0 copy-start.3
  2.0 0.0 copy-done.4
  2.0 0.7 copy-done.3
  2.6 0.0 copy-start.5
  2.7 0.6 copy-done.5
  3.3 0.1 copy.16.goal_ref
  3.4 0.0 copy-start
  3.4 1.0 copy-done
  4.4 0.0 copy-start.1
  4.4 0.9 copy-done.1
  5.3 0.0 copy-start.2
  5.3 0.9 copy-done.2
  6.2 87.1 %shard_map.143 = (f32[1,1]{1,0:T(1,128)}, f32[1,1]{1,0:T(1,128)}, f32[1,1]{1,0:T(1,128)}, f32[192,1152]{1,0:T(8,128)S(1)}, f32[1,1536]{1,0:T(1,128)S(1)}, /*inde...) custom-call(bf16[64,1536]{1,0:T(8,128)(2,1)S(1)} %copy-done.1, bf16[64,1152]{1,0:T(8,128)(2,1)S(1)} %copy-done.2, ...), custom_call_target="tpu_custom_call" | custom-call | tf_op jit(solution)/shard_map/pallas_call | solution.py:454
  93.3 0.6 reduce
  94.0 0.6 reduce.1
  96.5 0.9 copy.28
  97.4 0.7 copy.29
  98.1 0.7 copy.30
  (2 shorter events, 0.0 us)
Async XLA Ops:
  0.6 1.3 %copy-start.4 = (f32[1152]{0:T(1024)S(1)}, f32[1152]{0:T(1024)}, u32[]{:S(2)}) copy-start(f32[1152]{0:T(1024)} %param.13) | copy-start | bytes 13828
  1.9 0.7 copy-start.3
  2.6 0.7 copy-start.5
  3.4 1.0 copy-start
  4.4 0.9 copy-start.1
  5.3 0.9 copy-start.2

commit v2 on v1

--- a/solution.py
+++ b/solution.py
@@ -168,12 +168,13 @@
 
 
 def kernel(
-    batch_total, img_ref, txt_ref, goal_ref, part_ref, igain_ref, tgain_ref, scale_ref, bias_ref,
+    batch_total, img_hbm, txt_hbm, goal_ref, part_ref, igain_hbm, tgain_hbm, scale_ref, bias_ref,
     loss_ref, gscale_ref, gbias_ref, gproj_ref, gig_ref, gtg_ref, gif_ref, gtf_ref,
-    full_ref, norm_ref, hat_ref, turned_ref, turned_in, proj_ref,
+    img_ref, txt_ref, igain_ref, tgain_ref, full_ref, norm_ref, hat_ref, turned_ref, turned_in, proj_ref,
     txt_set, img_set, weight_ref, turnw_ref, block_ref, block_out, block_in,
     gtx_ref, gtx_out, gtx_in, gtz_out, gtz_in, grad_set,
-    gp_in, gp_out, gp_far, gp_sum, gp_end, small_ref, small_in, mid_ref, mid_in, send_sem, recv_sem,
+    gp_in, gp_out, gp_far, gp_sum, gp_end, small_ref, small_in, mid_ref, mid_in, back_ref,
+    load_sem, send_sem, recv_sem,
 ):
     rows = img_ref.shape[0]
     depth = part_ref.shape[0]
@@ -190,6 +191,15 @@
     def group(r):
         return flip(y, r & 2) * 2 + flip(core, r & 1)
 
+    own_rows = full_ref.at[pl.ds(pl.multiple_of(f * depth, 16), depth), :]
+    loads = []
+    for source, target in (
+        (txt_hbm, txt_ref), (tgain_hbm, tgain_ref), (img_hbm, img_ref), (igain_hbm, igain_ref),
+        (part_ref, own_rows),
+    ):
+        loads.append(pltpu.make_async_copy(source, target, load_sem.at[len(loads)]))
+        loads[-1].start()
+
     barrier = pltpu.get_barrier_semaphore()
     for r in range(1, 8):
         pl.semaphore_signal(barrier, inc=1, device_id=(b, member(r)), device_id_type=MESH)
@@ -223,8 +233,9 @@
     arrive = {}
     for r in (4, 6, 2, 1):
         arrive[r, 0] = send(own_piece, piece(0, 0), along(r))
-    full_ref[pl.ds(pl.multiple_of(f * depth, 16), depth), :] = part_ref[...]
-
+
+    loads[0].wait()
+    loads[1].wait()
     values = txt_ref[...].astype(F32)
     centered = values - jnp.mean(values, axis=1, keepdims=True)
     txt_inv = lax.rsqrt(jnp.mean(centered * centered, axis=1, keepdims=True) + EPSILON)
@@ -236,6 +247,17 @@
     for r in (4, 6, 2, 1):
         txt_arrive[r] = send(txt_set.at[txt_slot(0)], txt_set.at[txt_slot(r)], along(r))
 
+    def spread(r):
+        arrive[r, 0].wait_recv()
+        if r % 2 == 0:
+            arrive[r + 1, 0] = send(piece(r, 0), piece(r, 0), along(1))
+        arrive[r, 2] = send(piece(r, 0), piece(r, 0), across(2))
+        arrive[r, 1] = send(piece(r, 0), piece(r, 0), across(1))
+
+    spread(2)
+
+    loads[2].wait()
+    loads[3].wait()
     values = img_ref[...].astype(F32)
     centered = values - jnp.mean(values, axis=1, keepdims=True)
     img_inv = lax.rsqrt(jnp.mean(centered * centered, axis=1, keepdims=True) + EPSILON)
@@ -243,17 +265,11 @@
     hat_ref[...] = img_hat
     img_norm = img_hat * igain_ref[...]
     norm_ref[...] = img_norm.astype(BF16)
-    turned_ref[...] = jnp.transpose(img_norm).astype(BF16)
-
-    for r in (2, 4, 6):
-        arrive[r, 0].wait_recv()
-        arrive[r + 1, 0] = send(piece(r, 0), piece(r, 0), along(1))
-        arrive[r, 2] = send(piece(r, 0), piece(r, 0), across(2))
-        arrive[r, 1] = send(piece(r, 0), piece(r, 0), across(1))
+    for r in (4, 6):
+        spread(r)
+    turned_ref[...] = jnp.transpose(hat_ref[...] * igain_ref[...]).astype(BF16)
     for r in (1, 3, 5, 7):
-        arrive[r, 0].wait_recv()
-        arrive[r, 2] = send(piece(r, 0), piece(r, 0), across(2))
-        arrive[r, 1] = send(piece(r, 0), piece(r, 0), across(1))
+        spread(r)
     for r in (2, 4, 6):
         txt_arrive[r].wait_recv()
         txt_arrive[r + 1] = send(
@@ -262,6 +278,7 @@
     for r in (2, 4, 6, 1, 3, 5, 7):
         arrive[r, 2].wait_recv()
         arrive[r, 3] = send(piece(r, 2), piece(r, 2), across(1))
+    loads[4].wait()
     img_proj = None
     for r in (0, 2, 4, 6):
         for s in (r, r + 1):
@@ -342,12 +359,17 @@
         grad_arrive[r] = send(grad_set.at[0], grad_set.at[r], along(r))
 
     gtz_arrive = {}
+    third = full_ref.shape[0] // 3
     for k in (1, 2, 3):
         gtx_arrive[k - 1].wait_recv()
         gtz_out[k] = (gtx_ref[k] + gtx_in[k].astype(F32)).astype(BF16)
         gtz_arrive[k] = send(gtz_out.at[k], gtz_in.at[k], along(2 * k))
-
-    grad_norm = matmul_nt(grad_set[0], full_ref[...])
+        grad_arrive[2 * k].wait_recv()
+        grad_arrive[2 * k + 1] = send(grad_set.at[2 * k], grad_set.at[2 * k + 1], along(1))
+        part = slice((k - 1) * third, k * third)
+        back_ref[:, part] = matmul_nt(grad_set[0], full_ref[part, :])
+
+    grad_norm = back_ref[...]
     img_hat = hat_ref[...]
     img_gain_sum = jnp.sum(grad_norm * img_hat, axis=0, keepdims=True)
     scaled = grad_norm * igain_ref[...]
@@ -357,14 +379,11 @@
         - img_hat * jnp.mean(scaled * img_hat, axis=1, keepdims=True)
     )
 
-    for r in (2, 4, 6):
-        grad_arrive[r].wait_recv()
-        grad_arrive[r + 1] = send(grad_set.at[r], grad_set.at[r + 1], along(1))
-
     grad_proj = matmul(turned_in[0], grad_set[0])
     for r in (2, 4, 6):
         turned_arrive[r].wait_recv()
         grad_proj = grad_proj + matmul(turned_in[r], grad_set[r])
+    gproj_ref[...] = grad_proj
 
     gtx_arrive[3].wait_recv()
     grad = gtx_ref[0] + gtx_in[0].astype(F32)
@@ -399,11 +418,17 @@
     for r in (1, 3, 5, 7):
         turned_arrive[r].wait_recv()
         grad_arrive[r].wait_recv()
-        grad_proj = grad_proj + matmul(turned_in[r], grad_set[r])
-    gproj_ref[...] = grad_proj
     mine = pl.ds(pl.multiple_of(core * half, 16), half)
     other = pl.ds(pl.multiple_of((1 - core) * half, 16), half)
-    gp_first = send(gproj_ref.at[other, :], gp_in, across(1))
+    span_width = gproj_ref.shape[1] // 3
+    spans = [slice(k * span_width, (k + 1) * span_width) for k in range(3)]
+    gp_first = []
+    for k, span in enumerate(spans):
+        grad_proj = gproj_ref[:, span]
+        for r in (1, 3, 5, 7):
+            grad_proj = grad_proj + matmul(turned_in[r], grad_set[r, :, span])
+        gproj_ref[:, span] = grad_proj
+        gp_first.append(send(gproj_ref.at[other, span], gp_in.at[k], across(1)))
 
     small_in[b] = small_ref[...]
     for copy in small_arrive:
@@ -412,9 +437,17 @@
     mid_arrive = [send(mid_ref, mid_in.at[f], along(r)) for r in range(1, 8)]
     mid_in[f] = mid_ref[...]
 
-    gp_first.wait()
-    gp_out[...] = (gproj_ref[mine, :] + gp_in[...]).astype(BF16)
-    gp_step = send(gp_out, gp_far, across(2))
+    gp_second = []
+    for k, span in enumerate(spans):
+        gp_first[k].wait_recv()
+        gp_out[k] = (gproj_ref[mine, span] + gp_in[k]).astype(BF16)
+        gp_second.append(send(gp_out.at[k], gp_far.at[k], across(2)))
+    gp_third = []
+    for k, span in enumerate(spans):
+        gp_second[k].wait_recv()
+        gp_sum[k] = gp_out[k].astype(F32) + gp_far[k].astype(F32)
+        gp_third.append(send(gp_sum.at[k], gp_end.at[k], across(1)))
+        gproj_ref[mine, span] = gp_sum[k]
 
     for copy in mid_arrive:
         copy.wait_recv()
@@ -431,15 +464,13 @@
     gscale_ref[...] = sums[at:at + 1, 1:2]
     gbias_ref[...] = sums[at:at + 1, 2:3]
 
-    gp_step.wait_recv()
-    gp_sum[...] = gp_out[...].astype(F32) + gp_far[...].astype(F32)
-    gp_last = send(gp_sum, gp_end, across(1))
-    gproj_ref[mine, :] = gp_sum[...]
-    gp_last.wait_recv()
-    gproj_ref[other, :] = gp_end[...]
+    for k, span in enumerate(spans):
+        gp_third[k].wait_recv()
+        gp_first[k].wait_send()
+        gproj_ref[other, span] = gp_end[k]
 
     for copy in copies:
-        if copy is not gp_first:
+        if not any(copy is first for first in gp_first):
             copy.wait_send()
 
 
@@ -463,9 +494,15 @@
             jax.ShapeDtypeStruct((rows, width), F32),
             jax.ShapeDtypeStruct((rows, emb), F32),
         ),
-        in_specs=[pl.BlockSpec(memory_space=vmem)] * 8,
+        in_specs=[
+            pl.BlockSpec(memory_space=vmem if k in (2, 6, 7) else pl.ANY) for k in range(8)
+        ],
         out_specs=tuple([pl.BlockSpec(memory_space=vmem)] * 8),
         scratch_shapes=[
+            vmem((rows, width), BF16),
+            vmem((rows, emb), BF16),
+            vmem((1, width), F32),
+            vmem((1, emb), F32),
             vmem((width, emb), BF16),
             vmem((rows, width), BF16),
             vmem((rows, width), F32),
@@ -485,20 +522,22 @@
             vmem((4, rows, emb), BF16),
             vmem((4, rows, emb), BF16),
             vmem((8, rows, emb), BF16),
-            vmem((depth // 2, emb), F32),
-            vmem((depth // 2, emb), BF16),
-            vmem((depth // 2, emb), BF16),
-            vmem((depth // 2, emb), F32),
-            vmem((depth // 2, emb), F32),
+            vmem((3, depth // 2, emb // 3), F32),
+            vmem((3, depth // 2, emb // 3), BF16),
+            vmem((3, depth // 2, emb // 3), BF16),
+            vmem((3, depth // 2, emb // 3), F32),
+            vmem((3, depth // 2, emb // 3), F32),
             vmem((small_rows, 128), F32),
             vmem((4, small_rows, 128), F32),
             vmem((small_rows, 128), F32),
             vmem((8, small_rows, 128), F32),
-            pltpu.SemaphoreType.DMA((80,)),
-            pltpu.SemaphoreType.DMA((80,)),
+            vmem((rows, width), F32),
+            pltpu.SemaphoreType.DMA((5,)),
+            pltpu.SemaphoreType.DMA((90,)),
+            pltpu.SemaphoreType.DMA((90,)),
         ],
         compiler_params=pltpu.CompilerParams(
-            collective_id=0, has_side_effects=True, vmem_limit_bytes=48 * 1024 * 1024
+            collective_id=0, has_side_effects=True, vmem_limit_bytes=58 * 1024 * 1024
         ),
     )(
         img_feat,

time: 103 us -> 104 us (level)
  Pallas kernels: 87.1 us -> 88.3 us
    unnamed x15 -> x17, local copies, waits for them, and re-layouts: 6.54 us -> 4.91 us
    pallas_call x1, Pallas kernels: 87.1 us -> 88.3 us  [fused_shards(): pl.pallas_call(functools.partial(kernel, batch_total), out_shape=(scalar,...]
where the time goes in v2:
time: 104 us
  Pallas kernels  88.3 us (85%)
  between operations  7.32 us (7%)
  local copies, waits for them, and re-layouts  6.81 us (7%)
  other arithmetic  1.24 us (1%)
    pallas_call x1, Pallas kernels, fused_shards(): pl.pallas_call(functools.partial(kernel, batch_total), out_shape=(scalar,...  88.3 us
    unnamed x17, local copies, waits for them, and re-layouts  4.91 us

profile of v2, /device:TPU:17, one launch (start us, length us, event | category | flops | bytes accessed | tf_op | source)
XLA Modules:
  0.0 103.7 jit_solution(13868666078079102052)
XLA Ops:
  0.6 0.0 copy-start.3
  1.9 0.0 copy-start.2
  2.0 0.0 copy-done.3
  2.0 0.6 reshape.48.tgain_hbm
  2.6 0.1 copy-done.2
  2.6 0.0 copy-start.6
  2.6 0.6 reshape.47.igain_hbm
  3.2 0.1 copy-done.6
  3.3 0.7 copy.16.goal_ref
  4.0 88.3 %shard_map.143 = (f32[1,1]{1,0:T(1,128)}, f32[1,1]{1,0:T(1,128)}, f32[1,1]{1,0:T(1,128)}, f32[192,1152]{1,0:T(8,128)}, f32[1,1536]{1,0:T(1,128)}, /*index=5*/f32...) custom-call(bf16[64,1536]{1,0:T(8,128)(2,1)} %img_hbm.1, bf16[64,1152]{1,0:T(8,128)(2,1)} %txt_hbm.1, ...), custom_call_target="tpu_custom_call" | custom-call | tf_op jit(solution)/shard_map/pallas_call | solution.py:485
  92.3 0.0 copy-start.4
  92.3 0.7 copy-done.4
  93.0 0.0 copy-start.5
  93.0 0.6 reduce
  93.6 0.1 copy-done.5
  93.7 0.6 reduce.1
  96.3 0.0 copy-start
  96.3 2.2 %copy.28 = f32[192,1152]{1,0:T(8,128)} copy(f32[192,1152]{1,0:T(8,128)} %get-tuple-element.35) | data formatting | bytes 1769472
  98.5 0.0 copy-done
  98.5 0.0 copy-start.1
  98.5 0.7 copy.29
  99.2 0.4 copy-done.1
  99.6 0.7 copy.30
Async XLA Ops:
  0.6 1.3 %copy-start.3 = (f32[1152]{0:T(1024)S(1)}, f32[1152]{0:T(1024)}, u32[]{:S(2)}) copy-start(f32[1152]{0:T(1024)} %param.13) | copy-start | bytes 13828
  1.9 0.7 copy-start.2
  2.6 0.7 copy-start.6
  92.3 0.7 copy-start.4
  93.0 0.7 copy-start.5
  96.3 2.2 %copy-start = (f32[64,1536]{1,0:T(8,128)S(1)}, f32[64,1536]{1,0:T(8,128)}, u32[]{:S(2)}) copy-start(f32[64,1536]{1,0:T(8,128)} %get-tuple-element.38) | copy-start | bytes 1179652
  98.5 1.1 %copy-start.1 = (f32[64,1152]{1,0:T(8,128)S(1)}, f32[64,1152]{1,0:T(8,128)}, u32[]{:S(2)}) copy-start(f32[64,1152]{1,0:T(8,128)} %get-tuple-element.39) | copy-start | bytes 884740

commit v3 on v2

--- a/solution.py
+++ b/solution.py
@@ -168,7 +168,7 @@
 
 
 def kernel(
-    batch_total, img_hbm, txt_hbm, goal_ref, part_ref, igain_hbm, tgain_hbm, scale_ref, bias_ref,
+    batch_total, img_hbm, txt_hbm, goal_ref, part_ref, igain_flat, tgain_flat, scale_ref, bias_ref,
     loss_ref, gscale_ref, gbias_ref, gproj_ref, gig_ref, gtg_ref, gif_ref, gtf_ref,
     img_ref, txt_ref, igain_ref, tgain_ref, full_ref, norm_ref, hat_ref, turned_ref, turned_in, proj_ref,
     txt_set, img_set, weight_ref, turnw_ref, block_ref, block_out, block_in,
@@ -194,8 +194,7 @@
     own_rows = full_ref.at[pl.ds(pl.multiple_of(f * depth, 16), depth), :]
     loads = []
     for source, target in (
-        (txt_hbm, txt_ref), (tgain_hbm, tgain_ref), (img_hbm, img_ref), (igain_hbm, igain_ref),
-        (part_ref, own_rows),
+        (txt_hbm, txt_ref), (img_hbm, img_ref), (part_ref, own_rows),
     ):
         loads.append(pltpu.make_async_copy(source, target, load_sem.at[len(loads)]))
         loads[-1].start()
@@ -235,7 +234,8 @@
         arrive[r, 0] = send(own_piece, piece(0, 0), along(r))
 
     loads[0].wait()
-    loads[1].wait()
+    tgain_ref[...] = tgain_flat[...].reshape(tgain_ref.shape)
+    igain_ref[...] = igain_flat[...].reshape(igain_ref.shape)
     values = txt_ref[...].astype(F32)
     centered = values - jnp.mean(values, axis=1, keepdims=True)
     txt_inv = lax.rsqrt(jnp.mean(centered * centered, axis=1, keepdims=True) + EPSILON)
@@ -256,8 +256,7 @@
 
     spread(2)
 
-    loads[2].wait()
-    loads[3].wait()
+    loads[1].wait()
     values = img_ref[...].astype(F32)
     centered = values - jnp.mean(values, axis=1, keepdims=True)
     img_inv = lax.rsqrt(jnp.mean(centered * centered, axis=1, keepdims=True) + EPSILON)
@@ -278,7 +277,7 @@
     for r in (2, 4, 6, 1, 3, 5, 7):
         arrive[r, 2].wait_recv()
         arrive[r, 3] = send(piece(r, 2), piece(r, 2), across(1))
-    loads[4].wait()
+    loads[2].wait()
     img_proj = None
     for r in (0, 2, 4, 6):
         for s in (r, r + 1):
@@ -455,10 +454,10 @@
     for k in range(1, 8):
         sums = sums + mid_in[k]
     for k in range(img_tiles):
-        gig_ref[:, k * 128:(k + 1) * 128] = sums[k:k + 1, :]
+        gig_ref[k * 128:(k + 1) * 128] = sums[k]
     for k in range(txt_tiles):
         at = img_tiles + k
-        gtg_ref[:, k * 128:(k + 1) * 128] = sums[at:at + 1, :]
+        gtg_ref[k * 128:(k + 1) * 128] = sums[at]
     at = img_tiles + txt_tiles
     loss_ref[...] = sums[at:at + 1, 0:1] / batch_total
     gscale_ref[...] = sums[at:at + 1, 1:2]
@@ -489,13 +488,13 @@
             scalar,
             scalar,
             jax.ShapeDtypeStruct((depth, emb), F32),
-            jax.ShapeDtypeStruct((1, width), F32),
-            jax.ShapeDtypeStruct((1, emb), F32),
+            jax.ShapeDtypeStruct((width,), F32),
+            jax.ShapeDtypeStruct((emb,), F32),
             jax.ShapeDtypeStruct((rows, width), F32),
             jax.ShapeDtypeStruct((rows, emb), F32),
         ),
         in_specs=[
-            pl.BlockSpec(memory_space=vmem if k in (2, 6, 7) else pl.ANY) for k in range(8)
+            pl.BlockSpec(memory_space=pltpu.HBM if k in (0, 1, 3) else vmem) for k in range(8)
         ],
         out_specs=tuple([pl.BlockSpec(memory_space=vmem)] * 8),
         scratch_shapes=[
@@ -537,15 +536,15 @@
             pltpu.SemaphoreType.DMA((90,)),
         ],
         compiler_params=pltpu.CompilerParams(
-            collective_id=0, has_side_effects=True, vmem_limit_bytes=58 * 1024 * 1024
+            collective_id=0, has_side_effects=True, vmem_limit_bytes=48 * 1024 * 1024
         ),
     )(
         img_feat,
         txt_feat,
         partner.reshape(rows, 1),
         projection,
-        img_gain.reshape(1, width),
-        txt_gain.reshape(1, emb),
+        img_gain,
+        txt_gain,
         log_scale.reshape(1, 1),
         logit_bias.reshape(1, 1),
     )
@@ -555,8 +554,8 @@
         grad_scale.reshape(1),
         grad_bias.reshape(1),
         grad_proj,
-        img_sum.reshape(width),
-        txt_sum.reshape(emb),
+        img_sum,
+        txt_sum,
         img_grad,
         txt_grad,
     )

time: 104 us -> 103 us (level)
  other arithmetic: 1.24 us -> 0 us
    unnamed x17, local copies, waits for them, and re-layouts: 4.91 us -> 7.68 us
    pallas_call x2 -> x0, other arithmetic: 1.24 us -> none  [fused_shards(): pl.pallas_call(functools.partial(kernel, batch_total), out_shape=(scalar,...]
    reshape x2 -> x0, local copies, waits for them, and re-layouts: 1.19 us -> none  [the longest x1 0.6 us: fused_shards(): img_gain.reshape(1, width)]
where the time goes in v3:
time: 103 us; the launch traced here: 102 us
  Pallas kernels  87.4 us (85%)
  local copies, waits for them, and re-layouts  7.78 us (8%)
  between operations  7.26 us (7%)
    pallas_call x1, Pallas kernels, fused_shards(): pl.pallas_call(functools.partial(kernel, batch_total), out_shape=(scalar,...  87.4 us
    unnamed x17, local copies, waits for them, and re-layouts  7.68 us

profile of v3, /device:TPU:17, one launch (start us, length us, event | category | flops | bytes accessed | tf_op | source)
XLA Modules:
  0.0 102.5 jit_solution(622767811313035400)
XLA Ops:
  1.9 0.0 copy-start.5
  1.9 0.6 copy-done.5
  2.6 0.0 copy-start.3
  2.6 0.0 copy-start.4
  2.6 0.1 copy.16.goal_ref
  2.7 0.6 copy-done.3
  3.3 0.0 copy-done.4
  3.3 0.0 copy-start
  3.3 1.0 copy-done
  4.3 0.0 copy-start.1
  4.3 0.9 copy-done.1
  5.2 0.0 copy-start.2
  5.2 0.9 copy-done.2
  6.1 87.4 %shard_map.143 = (f32[1,1]{1,0:T(1,128)}, f32[1,1]{1,0:T(1,128)}, f32[1,1]{1,0:T(1,128)}, f32[192,1152]{1,0:T(8,128)S(1)}, f32[1536]{0:T(1024)S(1)}, /*index=5*/...) custom-call(bf16[64,1536]{1,0:T(8,128)(2,1)S(1)} %copy-done.1, bf16[64,1152]{1,0:T(8,128)(2,1)S(1)} %copy-done.2, ...), custom_call_target="tpu_custom_call" | custom-call | tf_op jit(solution)/shard_map/pallas_call | solution.py:484
  95.5 0.9 copy.30
  96.4 0.6 copy.31
  97.0 0.6 copy.32
  97.6 0.7 copy.33
  98.4 0.7 copy.34
Async XLA Ops:
  1.9 0.7 copy-start.5
  2.6 0.7 copy-start.3
  2.6 0.7 copy-start.4
  3.3 1.0 copy-start
  4.3 0.9 copy-start.1
  5.2 0.9 copy-start.2

commit v4 on v1

--- a/solution.py
+++ b/solution.py
@@ -168,9 +168,9 @@
 
 
 def kernel(
-    batch_total, img_ref, txt_ref, goal_ref, part_ref, igain_ref, tgain_ref, scale_ref, bias_ref,
+    batch_total, img_ref, txt_ref, goal_ref, part_ref, igain_flat, tgain_flat, scale_ref, bias_ref,
     loss_ref, gscale_ref, gbias_ref, gproj_ref, gig_ref, gtg_ref, gif_ref, gtf_ref,
-    full_ref, norm_ref, hat_ref, turned_ref, turned_in, proj_ref,
+    igain_ref, tgain_ref, full_ref, norm_ref, hat_ref, turned_ref, turned_in, proj_ref,
     txt_set, img_set, weight_ref, turnw_ref, block_ref, block_out, block_in,
     gtx_ref, gtx_out, gtx_in, gtz_out, gtz_in, grad_set,
     gp_in, gp_out, gp_far, gp_sum, gp_end, small_ref, small_in, mid_ref, mid_in, send_sem, recv_sem,
@@ -224,6 +224,9 @@
     for r in (4, 6, 2, 1):
         arrive[r, 0] = send(own_piece, piece(0, 0), along(r))
     full_ref[pl.ds(pl.multiple_of(f * depth, 16), depth), :] = part_ref[...]
+
+    tgain_ref[...] = tgain_flat[...].reshape(tgain_ref.shape)
+    igain_ref[...] = igain_flat[...].reshape(igain_ref.shape)
 
     values = txt_ref[...].astype(F32)
     centered = values - jnp.mean(values, axis=1, keepdims=True)
@@ -422,10 +425,10 @@
     for k in range(1, 8):
         sums = sums + mid_in[k]
     for k in range(img_tiles):
-        gig_ref[:, k * 128:(k + 1) * 128] = sums[k:k + 1, :]
+        gig_ref[k * 128:(k + 1) * 128] = sums[k]
     for k in range(txt_tiles):
         at = img_tiles + k
-        gtg_ref[:, k * 128:(k + 1) * 128] = sums[at:at + 1, :]
+        gtg_ref[k * 128:(k + 1) * 128] = sums[at]
     at = img_tiles + txt_tiles
     loss_ref[...] = sums[at:at + 1, 0:1] / batch_total
     gscale_ref[...] = sums[at:at + 1, 1:2]
@@ -458,14 +461,16 @@
             scalar,
             scalar,
             jax.ShapeDtypeStruct((depth, emb), F32),
-            jax.ShapeDtypeStruct((1, width), F32),
-            jax.ShapeDtypeStruct((1, emb), F32),
+            jax.ShapeDtypeStruct((width,), F32),
+            jax.ShapeDtypeStruct((emb,), F32),
             jax.ShapeDtypeStruct((rows, width), F32),
             jax.ShapeDtypeStruct((rows, emb), F32),
         ),
         in_specs=[pl.BlockSpec(memory_space=vmem)] * 8,
         out_specs=tuple([pl.BlockSpec(memory_space=vmem)] * 8),
         scratch_shapes=[
+            vmem((1, width), F32),
+            vmem((1, emb), F32),
             vmem((width, emb), BF16),
             vmem((rows, width), BF16),
             vmem((rows, width), F32),
@@ -505,8 +510,8 @@
         txt_feat,
         partner.reshape(rows, 1),
         projection,
-        img_gain.reshape(1, width),
-        txt_gain.reshape(1, emb),
+        img_gain,
+        txt_gain,
         log_scale.reshape(1, 1),
         logit_bias.reshape(1, 1),
     )
@@ -516,8 +521,8 @@
         grad_scale.reshape(1),
         grad_bias.reshape(1),
         grad_proj,
-        img_sum.reshape(width),
-        txt_sum.reshape(emb),
+        img_sum,
+        txt_sum,
         img_grad,
         txt_grad,
     )

time: 103 us -> 102 us (level)
  other arithmetic: 1.24 us -> 0 us
  local copies, waits for them, and re-layouts: 6.65 us -> 7.78 us
    pallas_call x2 -> x0, other arithmetic: 1.24 us -> none  [fused_shards(): pl.pallas_call(functools.partial(kernel, batch_total), out_shape=(scalar,...]
    unnamed x15 -> x17, local copies, waits for them, and re-layouts: 6.54 us -> 7.68 us
where the time goes in v4:
time: 102 us
  Pallas kernels  87.1 us (85%)
  local copies, waits for them, and re-layouts  7.78 us (8%)
  between operations  7.26 us (7%)
    pallas_call x1, Pallas kernels, fused_shards(): pl.pallas_call(functools.partial(kernel, batch_total), out_shape=(scalar,...  87.1 us
    unnamed x17, local copies, waits for them, and re-layouts  7.68 us

profile of v4, /device:TPU:17, one launch (start us, length us, event | category | flops | bytes accessed | tf_op | source)
XLA Modules:
  0.0 102.2 jit_solution(18199248819130731072)
XLA Ops:
  1.9 0.0 copy-start.5
  1.9 0.6 copy-done.5
  2.6 0.0 copy-start.3
  2.6 0.0 copy-start.4
  2.6 0.1 copy.16.goal_ref
  2.7 0.6 copy-done.3
  3.3 0.0 copy-done.4
  3.3 0.0 copy-start
  3.3 1.0 copy-done
  4.3 0.0 copy-start.1
  4.3 0.9 copy-done.1
  5.2 0.0 copy-start.2
  5.2 0.9 copy-done.2
  6.1 87.1 %shard_map.143 = (f32[1,1]{1,0:T(1,128)}, f32[1,1]{1,0:T(1,128)}, f32[1,1]{1,0:T(1,128)}, f32[192,1152]{1,0:T(8,128)S(1)}, f32[1536]{0:T(1024)S(1)}, /*index=5*/...) custom-call(bf16[64,1536]{1,0:T(8,128)(2,1)S(1)} %copy-done.1, bf16[64,1152]{1,0:T(8,128)(2,1)S(1)} %copy-done.2, ...), custom_call_target="tpu_custom_call" | custom-call | tf_op jit(solution)/shard_map/pallas_call | solution.py:457
  95.2 0.9 copy.30
  96.1 0.6 copy.31
  96.7 0.6 copy.32
  97.3 0.7 copy.33
  98.1 0.7 copy.34
Async XLA Ops:
  1.9 0.7 copy-start.5
  2.6 0.7 copy-start.3
  2.6 0.7 copy-start.4
  3.3 1.0 copy-start
  4.3 0.9 copy-start.1
  5.2 0.9 copy-start.2
